TPU v7x, 256 devices: a whole 4x4x8 slice. The times are simulated.
256 devices in a mesh: gx: 32 (over z_lo, x, core), gy: 8 (over z_hi, y).
Axes of the slice: x: 4, y: 4, z: 8 (z_hi: 2, z_lo: 4; z = z_hi * 4 + z_lo), core: 2. Of those that a mesh axis runs over, the one named last changes fastest.
Arguments:
- input_field: bfloat16 [1, 32, 192, 256, 256], P(None, None, 'gx', 'gy'), may hold values from -6 to 6
- cotangent: bfloat16 [1, 32, 192, 256, 256], P(None, None, 'gx', 'gy'), may hold values from -6 to 6
- spectral_weights: float32 [2, 17, 48, 64, 1024], P(None, None, 'gy', 'gx'), may hold values from -6 to 6
- point_weight: bfloat16 [32, 32], replicated, may hold values from -1 to 1
- point_bias: float32 [32], replicated, may hold values from -1 to 1
Outputs:
- input_grad: bfloat16 [1, 32, 192, 256, 256], P(None, None, 'gx', 'gy')
- weight_grad: float32 [2, 17, 48, 64, 1024], P(None, None, 'gy', 'gx')
All inputs are finite; a program needn't handle non-finite values.
Results may differ from a plain program's by a relative error of at most 0.0052.
Values sent between devices are 32-bit elements; how exact they have to be, the bound alone decides.
A program may use at most 128 MiB of HBM per device.

v0:
```python
import math

import jax
import jax.numpy as jnp
import ml_dtypes
import numpy as np
from jax import lax
from jax.experimental import pallas as pl
from jax.experimental.pallas import tpu as pltpu
from jax.sharding import PartitionSpec as P

C = 32
NX = 192
NY = 256
NZ = 256
KX = 48
KY = 64
KZ = 17
SCALE = (NX * NY * NZ) ** (-0.5)
MESH = pl.DeviceIdType.MESH
F32 = jnp.float32
BF16 = jnp.bfloat16


def kept(count, number):
    half = number // 2
    return np.concatenate([np.arange(half), np.arange(half) + count - half])


def trig(points, freqs, count):
    angle = 2.0 * np.pi * ((points[:, None] * freqs[None, :]) % count) / count
    return np.cos(angle), np.sin(angle)


def hi_lo(table):
    table = np.asarray(table, np.float32)
    high = table.astype(ml_dtypes.bfloat16)
    low = (table - high.astype(np.float32)).astype(ml_dtypes.bfloat16)
    return high, low


def make_tables():
    z_cos, z_sin = trig(np.arange(NZ), np.arange(KZ), NZ)
    y_cos, y_sin = trig(np.arange(NY), kept(NY, KY), NY)
    x_cos, x_sin = trig(np.arange(NX), kept(NX, KX), NX)
    tabs = {}
    wz = np.zeros((4, NZ, 2, 2, 4, 16))
    zz = np.zeros((4, 2, 2, 4, 16, NZ))
    for c4 in range(4):
        wz[c4, :, 0, 0, c4, :] = z_cos[:, :16]
        wz[c4, :, 0, 1, c4, :] = -z_sin[:, :16]
        wz[c4, :, 1, 0, c4, :] = z_cos[:, 16:17]
        wz[c4, :, 1, 1, c4, :] = -z_sin[:, 16:17]
        zz[c4, 0, 0, c4] = z_cos[:, :16].T
        zz[c4, 0, 1, c4] = -z_sin[:, :16].T
        zz[c4, 1, 0, c4] = z_cos[:, 16:17].T
        zz[c4, 1, 1, c4] = -z_sin[:, 16:17].T
    tabs["wz"] = wz.reshape(4 * NZ, 256).astype(np.float32).astype(ml_dtypes.bfloat16)
    tabs["zz"] = hi_lo(zz.reshape(4, 256, NZ))[0]
    s_at, zl_at, j_at = np.meshgrid(np.arange(8), np.arange(4), np.arange(2), indexing="ij")
    order = ((zl_at * 8 + s_at) * 2 + j_at).reshape(-1)
    yc = (y_cos * SCALE)[:, order].reshape(2, 128, 64)
    ys = (y_sin * SCALE)[:, order].reshape(2, 128, 64)
    inv = np.concatenate([yc, ys], 2)
    fwd = inv.transpose(0, 2, 1)
    tabs["t1"] = np.stack([np.concatenate([h, h, l], -1) for h, l in [hi_lo(fwd[0]), hi_lo(fwd[1])]])
    tabs["t1i"] = np.stack([np.concatenate([h, h, l], -1) for h, l in [hi_lo(inv[0]), hi_lo(inv[1])]])
    xt = np.stack([x_cos, x_sin]).reshape(2, 4, 8, 6, 2, 4, 6)
    t2 = np.zeros((4, 2, 4, 2, 4, 16, 6, 8, 8))
    for zl_to in range(4):
        for i in range(6):
            for j in range(2):
                block = xt[:, :, :, :, :, :, i]
                t2[:, :, zl_to, :, :, 2 * i + j, :, :, zl_to * 2 + j] = block.transpose(1, 4, 0, 5, 3, 2)
    fwd = t2.reshape(4, 8, 128, 384)
    tabs["t2"] = np.concatenate(hi_lo(fwd), 3)
    inv = t2.transpose(0, 6, 3, 7, 8, 1, 2, 4, 5).reshape(4, 6, 128, 512)
    tabs["t2i"] = np.concatenate(hi_lo(inv), 2)
    eye2, eye4 = np.eye(2), np.eye(4)
    ones16, ones32 = np.ones(16), np.ones(32)
    e1 = np.einsum("qr,cd,s,o->qcsrdo", eye2, eye4, ones16, ones32)
    tabs["e1"] = e1.reshape(128, 256)
    tabs["r2"] = e1.reshape(128, 256).T
    pick = np.eye(32).reshape(8, 4, 32)
    e2 = np.einsum("qr,bio,s,c->bqisrco", eye2, pick, ones16, np.ones(4)).reshape(8, 128, 256)
    tabs["e2"] = e2
    tabs["rr"] = e2.reshape(2, 2, 2, 128, 256).transpose(2, 0, 4, 1, 3).reshape(2, 2, 256, 256)
    slot = np.zeros((6, 16, 16))
    for x in range(6):
        slot[x, x, :] = 1.0
    spread = np.einsum("qr,cd,xst->xqcsrdt", eye2, eye4, slot).reshape(6, 128, 128)
    tabs["spread"] = spread.transpose(1, 0, 2).reshape(128, 768)
    tabs["gather"] = spread.transpose(0, 2, 1)
    tabs["a16"] = np.repeat(np.eye(32), 16, axis=0)
    for name in ("e1", "r2", "e2", "rr", "spread", "gather", "a16"):
        tabs[name] = tabs[name].astype(ml_dtypes.bfloat16)
    return tabs


TABLES = make_tables()
IN_VMEM = ("wz", "t1", "a16", "spread", "gather", "t1i", "e1", "r2")
IN_HBM = ("t2", "t2i", "zz", "e2", "rr")


def mm(left, right):
    return jnp.dot(left, right, preferred_element_type=F32)


def halves(values):
    high = values.astype(BF16)
    return high, (values - high.astype(F32)).astype(BF16)


def gelu_slope(values):
    size = jnp.abs(values)
    below = 1.0 + (0.3275911 / math.sqrt(2.0)) * size
    t = pl.reciprocal(below, approx=True)
    t = t * (2.0 - below * t)
    poly = t * (0.127414796 + t * (-0.142248368 + t * (0.7107068705 + t * (-0.7265760135 + t * 0.5307027145))))
    bell = jnp.exp2((-0.5 / math.log(2.0)) * (values * values))
    part = bell * (poly - (1.0 / math.sqrt(2.0 * math.pi)) * size)
    return jnp.where(values >= 0.0, 1.0 - part, part)


def swap(values, first):
    lane = lax.broadcasted_iota(jnp.int32, (values.shape[0], 128), 1)
    sign = jnp.where(lane < 64, first, -first)
    parts = [
        pltpu.roll(values[:, at : at + 128], 64, 1) * sign for at in range(0, values.shape[1], 128)
    ]
    return parts[0] if len(parts) == 1 else jnp.concatenate(parts, 1)


def slot_of(shape):
    return jnp.bitwise_and(lax.broadcasted_iota(jnp.int32, shape, len(shape) - 1), 15)


def row_of(shape):
    return jnp.bitwise_and(lax.broadcasted_iota(jnp.int32, shape, 0), 15)


def spread_rows(block):
    slots = slot_of((16, 128))
    rows = lax.broadcasted_iota(jnp.int32, (16, 128), 0)
    parts = [jnp.where(slots == k, block, 0.0) for k in range(16)]
    parts.append(jnp.where(slots == rows, jnp.broadcast_to(block[12:13], (16, 128)), 0.0))
    return jnp.concatenate(parts, 0)


def gather_rows(values):
    slots = slot_of((16, 128))
    rows = lax.broadcasted_iota(jnp.int32, (16, 128), 0)
    total = jnp.where(slots == 0, values[0:16], 0.0)
    for k in range(1, 16):
        total = total + jnp.where(slots == k, values[16 * k : 16 * k + 16], 0.0)
    last = jnp.sum(jnp.where(slots == rows, values[256:272], 0.0), axis=0, keepdims=True)
    return jnp.where(rows == 12, jnp.broadcast_to(last, (16, 128)), total)


def split_left(values, table):
    high, low = halves(values)
    out = mm(jnp.concatenate([high, low], 0), table)
    return out[: values.shape[0]] + out[values.shape[0] :]


GROUPS = ((0, 512), (512, 384))
CHUNKS = (((0, 256), (256, 256)), ((512, 256), (768, 128)))
ROWS = 13


def body(
    pw, bias, wz, t1, a16, spread, gather, t1i, e1, r2,
    t2_hbm, t2i_hbm, zz_hbm, e2_hbm, rr_hbm, f_hbm, cot_hbm, w_hbm,
    ig, wg_out,
    t2, t2i, zz, e2, rr, f, cot, w_in, w, wg, pg, lin, kron,
    u, r0, vs, r1, rsb, r3a, md, xb, mexp, gexp, acc,
    mq, r3b, xb2, vs2, r1s, ys, r0s, zb,
    f_sem, local_sem, s1s, s1r, s2s, s2r, s3s, s3r, g3s, g3r, g2s, g2r, g1s, g1r,
):
    gx = lax.axis_index("gx")
    gy = lax.axis_index("gy")
    zl, s = lax.div(gx, 8), lax.rem(gx, 8)
    zh, yy = lax.div(gy, 4), lax.rem(gy, 4)
    me = (zh * 4 + zl) * 4 + yy

    def y_id(to):
        return (gx, zh * 4 + to)

    def s_id(to):
        return (zl * 8 + to, gy)

    def m_id(zl_to, zh_to, y_to):
        return (zl_to * 8 + s, zh_to * 4 + y_to)

    def others(first):
        def one(z, y):
            pl.when(me != z * 4 + y)(lambda: first(z, z % 4, z // 4, y))

        for z in range(8):
            for y in range(4):
                one(z, y)

    def y_at(d):
        return lax.rem(yy + d, 4)

    def s_at(d):
        return lax.rem(s + d, 8)

    def each(low, high, fn):
        def step(d, carry):
            fn(d)
            return carry

        lax.fori_loop(low, high, step, 0)

    def f_load(to, h):
        return pltpu.make_async_copy(f_hbm.at[to, h], f.at[to, h], f_sem.at[to, h])

    for h in range(2):
        each(1, 5, lambda d, h=h: f_load(y_at(d), h).start())

    barrier = pltpu.get_barrier_semaphore()

    r3a[:, :, 8:16, :] = jnp.zeros((2, 32, 8, 128), F32)
    r3b[:, :, 8:16, :] = jnp.zeros((2, 32, 8, 128), F32)

    def greet(device):
        pl.semaphore_signal(barrier, inc=1, device_id=device, device_id_type=MESH)

    for d in range(1, 8):
        greet(s_id(s_at(d)))
    others(lambda z, zl_to, zh_to, y: greet(m_id(zl_to, zh_to, y)))

    loads = [
        pltpu.make_async_copy(src, dst, local_sem.at[n])
        for n, (src, dst) in enumerate(
            [
                (w_hbm, w_in),
                (t2_hbm.at[zl], t2),
                (rr_hbm, rr),
                (t2i_hbm.at[zl], t2i),
                (cot_hbm, cot),
                (zz_hbm, zz),
                (e2_hbm, e2),
            ]
        )
    ]
    for load in loads:
        load.start()
    def send(src, dst, send_sem, recv_sem, device):
        return pltpu.make_async_remote_copy(src, dst, send_sem, recv_sem, device_id=device, device_id_type=MESH)

    def c1(h, to, g):
        cells = pl.ds(*GROUPS[g])
        return send(u.at[h, to, :, cells], r0.at[h, yy, :, cells], s1s.at[h], s1r.at[h, g], y_id(to))

    def c2(h, to, g):
        cells = pl.ds(*GROUPS[g])
        return send(vs.at[h, to, :, cells], r1.at[h, s, :, cells], s2s.at[h], s2r.at[h], s_id(to))

    def c3(h, z, device_y):
        rows = pl.ds(0, ROWS)
        device = m_id(lax.rem(z, 4), lax.div(z, 4), device_y)
        return send(rsb.at[h, z * 4 + device_y, rows], r3a.at[h, me, rows], s3s.at[h], s3r.at[h], device)

    def k3(h, zl_to, zh_to, y):
        rows = pl.ds(0, ROWS)
        device = m_id(zl_to, zh_to, y)
        return send(mq.at[h, y, rows], r3b.at[h, me, rows], g3s.at[h], g3r.at[h], device)

    def k2(h, to, g):
        cells = pl.ds(*GROUPS[g])
        return send(vs2.at[h, to, :, cells], r1s.at[h, s, :, cells], g2s.at[h], g2r.at[h, g], s_id(to))

    def k1(h, to, g):
        cells = pl.ds(*GROUPS[g])
        return send(ys.at[h, to, :, cells], r0s.at[h, yy, :, cells], g1s.at[h], g1r.at[h, yy], y_id(to))

    def whole(part, sem):
        pltpu.make_async_copy(part, part, sem).wait()

    def all_of(buffer, h, count, sem):
        whole(buffer.at[h, pl.ds(0, count)], sem.at[h])

    def all_of_group(buffer, h, count, sem, g):
        whole(buffer.at[h, pl.ds(0, count), :, pl.ds(*GROUPS[g])], sem.at[h, g])

    def all_modes(buffer, h, sem):
        whole(buffer.at[h, pl.ds(0, 31), pl.ds(0, ROWS)], sem.at[h])

    def z_analysis(source, h, to, dest):
        total = mm(jnp.concatenate([source[to, h, q].reshape(192, 256) for q in range(4)], 1), wz[...])
        slots = slot_of((32, 128))
        last = None
        for x in range(6):
            rows = total[32 * x : 32 * x + 32]
            dest[:, 128 * x : 128 * x + 128] = rows[:, :128]
            part = jnp.where(slots == x, rows[:, 128:], 0.0)
            last = part if last is None else last + part
        dest[:, 768:896] = last

    def analysis_start(source, h, greeted):
        def one(d):
            to = y_at(d)
            f_load(to, h).wait()
            z_analysis(source, h, to, u.at[h, to])
            if greeted:
                c1(h, to, 0).start()

        each(1, 4, one)
        if not greeted:
            pl.semaphore_wait(barrier, 38)
            for d in range(1, 4):
                c1(h, y_at(d), 0).start()
        for d in range(1, 4):
            c1(h, y_at(d), 1).start()
        f_load(yy, h).wait()
        z_analysis(source, h, yy, r0.at[h, yy])

    def y_analysis(h, g):
        table = t1.at[zh]
        for at, wide in CHUNKS[g]:
            high, low = halves(r0[h, :, :, at : at + wide].reshape(128, wide))
            out = mm(table[...], jnp.concatenate([high, low, high], 0))
            vs[h, :, :, at : at + wide] = (out[:64] + swap(out[64:], 1.0)).reshape(8, 8, wide)

    def x_analysis_load(h):
        last = r1[h, :, :, 768:896].reshape(64, 128).astype(BF16)
        last = mm(last, spread[...]).astype(BF16)
        for x in range(6):
            at = 128 * x
            xb[64 * x : 64 * x + 64, 0:128] = r1[h, :, :, at : at + 128].reshape(64, 128).astype(BF16)
            xb[64 * x : 64 * x + 64, 128:256] = last[:, at : at + 128]

    def x_analysis_store(out, h, z):
        out = out[:64] + swap(out[64:], 1.0)
        rows = row_of((64, 128))
        last = jnp.where(slot_of((64, 128)) == rows, out[:, 128:], 0.0)
        last = jnp.sum(last.reshape(4, 16, 128), axis=1, keepdims=True)
        last = jnp.broadcast_to(last, (4, 16, 128)).reshape(64, 128)
        rsb[h, pl.ds(4 * z, 4)] = jnp.where(rows == 12, last, out[:, :128]).reshape(4, 16, 128)

    def x_analysis(h):
        mine = zh * 4 + zl
        for group in ((1, 2, 3, 4), (5, 6, 7, 8)):
            to = [lax.rem(mine + d, 8) for d in group]
            values = xb[...]
            out = mm(jnp.concatenate([t2[z] for z in to], 0), jnp.concatenate([values, values], 0))
            for n, d in enumerate(group):
                x_analysis_store(out[128 * n : 128 * n + 128], h, to[n])
                for y in range(4 if d < 8 else 3):
                    c3(h, to[n], y if d < 8 else y_at(y + 1)).start()
        r3a[h, me] = rsb[h, me]

    def analysis(first, second, received):
        first()
        for h in range(2):
            for g in range(2):
                all_of_group(r0, h, 3, s1r, g)
                y_analysis(h, g)
                for d in range(1, 8):
                    c2(h, s_at(d), g).start()
            r1[h, s] = vs[h, s]
        for h in range(2):
            all_of(r1, h, 7, s2r)
            x_analysis_load(h)
            x_analysis(h)
        second()
        for h in range(2):
            all_modes(r3a, h, s3r)
            total = r3a[h, 0:4]
            for z in range(1, 8):
                total = total + r3a[h, 4 * z : 4 * z + 4]
            md[h] = total
            received(h)

    def analysis_end():
        for h in range(2):
            all_of(u, h, 3, s1s)
            all_of(vs, h, 7, s2s)
            all_modes(rsb, h, s3s)

    def x_synthesis_load(h):
        main = r3b[h]
        rows = row_of((512, 128))
        last = jnp.broadcast_to(main[:, 12:13], (32, 16, 128)).reshape(512, 128)
        xb2[:, 0:128] = main.reshape(512, 128).astype(BF16)
        xb2[:, 128:256] = jnp.where(slot_of((512, 128)) == rows, last, 0.0).astype(BF16)

    def x_synthesis(h):
        total = None
        for group in ((0, 1), (2, 3), (4, 5)):
            out = mm(jnp.concatenate([t2i[x] for x in group], 0), xb2[...])
            for n, x in enumerate(group):
                part = out[256 * n : 256 * n + 128] + out[256 * n + 128 : 256 * n + 256]
                part = part[:64] + swap(part[64:], -1.0)
                vs2[h, :, :, 128 * x : 128 * x + 128] = part[:, :128].reshape(8, 8, 128)
                high, low = halves(part[:, 128:])
                last = mm(high, gather[x]) + mm(low, gather[x])
                total = last if total is None else total + last
            if group == (2, 3):
                for d in range(1, 8):
                    k2(h, s_at(d), 0).start()
        vs2[h, :, :, 768:896] = total.reshape(8, 8, 128)
        for d in range(1, 8):
            k2(h, s_at(d), 1).start()

    def y_synthesis(h, g):
        table = t1i.at[zh]
        for at, wide in CHUNKS[g]:
            values = r1s[h, :, :, at : at + wide].reshape(64, wide)
            high, low = halves(jnp.concatenate([values, swap(values, -1.0)], 0))
            out = mm(table[...], jnp.concatenate([high, low, high], 0))
            ys[h, :, :, at : at + wide] = out.reshape(4, 32, wide)

    def z_synthesis(h, fr, finish):
        slots = slot_of((32, 128))
        last = r0s[h, fr, :, 768:896]
        for x in range(6):
            zb[32 * x : 32 * x + 32, 0:128] = r0s[h, fr, :, 128 * x : 128 * x + 128].astype(BF16)
            zb[32 * x : 32 * x + 32, 128:256] = jnp.where(slots == x, last, 0.0).astype(BF16)

        def one(pair):
            for n in range(2):
                q = 2 * pair + n
                finish(fr, h, q, mm(zb[...], zz[q]).reshape(6, 32, 256))

        each(0, 2, one)

    def synthesis(meanwhile, finish, own, after):
        meanwhile()
        for h in range(2):
            all_modes(r3b, h, g3r)
            x_synthesis_load(h)
            x_synthesis(h)
            r1s[h, s] = vs2[h, s]
        for h in range(2):
            for g in range(2):
                all_of_group(r1s, h, 7, g2r, g)
                y_synthesis(h, g)
                for d in range(1, 4):
                    k1(h, y_at(d), g).start()
            r0s[h, yy] = ys[h, yy]
        for h in range(2):
            z_synthesis(h, yy, finish)
            own(h)
        for h in range(2):

            def one(d, h=h):
                fr = y_at(2 * d - 1 - lax.div(d, 3) * 3)
                whole(r0s.at[h, fr], g1r.at[h, fr])
                z_synthesis(h, fr, finish)
                after(h, fr)

            each(1, 4, one)
        for h in range(2):
            all_modes(r3b, h, g3s)
            all_of(vs2, h, 7, g2s)
            all_of(ys, h, 3, g1s)

    def channel_map(wide, source):
        rows = row_of((512, 512))
        columns = slot_of((512, 512))
        full = lax.dot_general(
            wide.astype(BF16), a16[...], (((1,), (1,)), ((), ())), preferred_element_type=F32
        )
        kron[...] = jnp.where(rows == columns, full, 0.0).astype(BF16)

        def one(x):
            for at in (0, 16):
                block = source[:, :, :, x, at : at + 16, :].reshape(512, 256)
                out = mm(kron[...], block)
                lin[:, :, :, x, at : at + 16, :] = out.reshape(4, 2, 4, 16, 256)

        each(0, 6, one)

    def lanes(b):
        return pl.ds(pl.multiple_of(b * 128, 128), 128)

    def weights_in():
        loads[0].wait()

        def one(k):
            for part in range(2):
                for i in range(6):
                    w[part, k, 2 * i : 2 * i + 2, :] = w_in[part, k, i]
                w[part, k, 12:16, :] = jnp.zeros((4, 1024), F32)

        each(0, KZ, one)

    def weight_grad_out():
        def one(k):
            for part in range(2):
                for i in range(6):
                    wg_out[part, k, i] = wg[part, k, 2 * i : 2 * i + 2, :]

        each(0, KZ, one)

    def w_at(part, b):
        return w[part, :, :, lanes(b)].reshape(272, 128)

    def mix_one(h):
        def one(y):
            b = 2 * y + h
            modes = split_left(spread_rows(md[h, y]), e1[...])
            mexp[b] = modes
            real, imag = modes[:, :128], modes[:, 128:]
            w_real, w_imag = w_at(0, b), w_at(1, b)
            acc[:, :128] += w_real * real - w_imag * imag
            acc[:, 128:] += w_real * imag + w_imag * real

        each(0, 4, one)

    def spread_out(h, y):
        def one(z):
            pl.when(me != z * 4 + y)(lambda: k3(h, z % 4, z // 4, y).start())

        for z in range(8):
            one(z)

    def keep_own(h):
        r3b[h, me] = mq[h, yy]

    def mix_two():
        for h in range(2):
            for pair in range(2):
                out = split_left(acc[...], rr[h, pair])
                for n in range(2):
                    y = 2 * pair + n
                    mq[h, y] = gather_rows(out[:, 128 * n : 128 * n + 128])
                    spread_out(h, y)
            keep_own(h)

    def back_one(h):
        def one(y):
            gexp[...] += split_left(spread_rows(md[h, y]), e2[2 * y + h])

        each(0, 4, one)

    def back_two():
        for h in range(2):

            def two(y, h=h):
                b = 2 * y + h
                g_real, g_imag = gexp[:, :128], gexp[:, 128:]
                w_real, w_imag = w_at(0, b), w_at(1, b)
                real = w_real * g_real + w_imag * g_imag
                imag = w_real * g_imag - w_imag * g_real
                mq[h, y] = gather_rows(split_left(jnp.concatenate([real, imag], 1), r2[...]))
                spread_out(h, y)

            each(0, 4, two)
            keep_own(h)

    def weight_grad():
        def one(b):
            g_real, g_imag = gexp[:, :128], gexp[:, 128:]
            real, imag = mexp[b, :, :128], mexp[b, :, 128:]
            wg[0, :, :, lanes(b)] = (real * g_real + imag * g_imag).reshape(KZ, 16, 128)
            wg[1, :, :, lanes(b)] = (real * g_imag - imag * g_real).reshape(KZ, 16, 128)

        each(0, 8, one)
        weight_grad_out()

    def finish_pre(fr, h, q, spectral):
        pre = spectral + lin[fr, h, q] + bias[fr * 8 + h * 4 + q]
        pg[fr, h, q] = (cot[fr, h, q].astype(F32) * gelu_slope(pre)).astype(BF16)

    def finish_grad(fr, h, q, spectral):
        ig[fr, h, q] = (spectral + lin[fr, h, q]).astype(BF16)

    def second_own(h):
        z_analysis(pg, h, yy, r0.at[h, yy])

    def second_start(h, to):
        z_analysis(pg, h, to, u.at[h, to])
        for g in range(2):
            c1(h, to, g).start()

    def first_y_wait():
        channel_map(mm(a16[...], pw[...]), f)
        loads[1].wait()

    def first_z_wait():
        weights_in()
        acc[...] = jnp.zeros_like(acc)

    def second_z_wait():
        wide = lax.dot_general(a16[...], pw[...], (((1,), (1,)), ((), ())), preferred_element_type=F32)
        channel_map(wide, pg)
        gexp[...] = jnp.zeros_like(gexp)

    def wait_loads():
        for load in loads[3:]:
            load.wait()

    for h in range(2):
        analysis_start(f, h, h == 1)
    analysis(first_y_wait, first_z_wait, mix_one)
    loads[2].wait()
    mix_two()
    analysis_end()
    synthesis(wait_loads, finish_pre, second_own, second_start)
    analysis(lambda: None, second_z_wait, back_one)
    back_two()
    synthesis(weight_grad, finish_grad, lambda h: None, lambda h, fr: None)
    analysis_end()


def per_device(input_field, cotangent, spectral_weights, point_weight, point_bias):
    field_shape = (4, 2, 4, 6, 32, 256)
    w_shape = spectral_weights.shape
    tabs = {name: jnp.asarray(value) for name, value in TABLES.items()}
    vmem = pl.BlockSpec(memory_space=pltpu.VMEM)
    smem = pl.BlockSpec(memory_space=pltpu.SMEM)
    hbm = pl.BlockSpec(memory_space=pl.ANY)
    dma = pltpu.SemaphoreType.DMA
    scratch = [
        pltpu.VMEM((8, 128, 768), BF16),
        pltpu.VMEM((6, 256, 512), BF16),
        pltpu.VMEM((4, 256, 256), BF16),
        pltpu.VMEM((8, 128, 256), BF16),
        pltpu.VMEM((2, 2, 256, 256), BF16),
        pltpu.VMEM(field_shape, BF16),
        pltpu.VMEM(field_shape, BF16),
        pltpu.VMEM(w_shape, F32),
        pltpu.VMEM((2, KZ, 16, 1024), F32),
        pltpu.VMEM((2, KZ, 16, 1024), F32),
        pltpu.VMEM(field_shape, BF16),
        pltpu.VMEM(field_shape, F32),
        pltpu.VMEM((512, 512), BF16),
        pltpu.VMEM((2, 4, 32, 896), F32),
        pltpu.VMEM((2, 4, 32, 896), F32),
        pltpu.VMEM((2, 8, 8, 896), F32),
        pltpu.VMEM((2, 8, 8, 896), F32),
        pltpu.VMEM((2, 32, 16, 128), F32),
        pltpu.VMEM((2, 32, 16, 128), F32),
        pltpu.VMEM((2, 4, 16, 128), F32),
        pltpu.VMEM((384, 256), BF16),
        pltpu.VMEM((8, 272, 256), F32),
        pltpu.VMEM((272, 256), F32),
        pltpu.VMEM((272, 256), F32),
        pltpu.VMEM((2, 4, 16, 128), F32),
        pltpu.VMEM((2, 32, 16, 128), F32),
        pltpu.VMEM((512, 256), BF16),
        pltpu.VMEM((2, 8, 8, 896), F32),
        pltpu.VMEM((2, 8, 8, 896), F32),
        pltpu.VMEM((2, 4, 32, 896), F32),
        pltpu.VMEM((2, 4, 32, 896), F32),
        pltpu.VMEM((192, 256), BF16),
        dma((4, 2)),
        dma((7,)),
        dma((2,)), dma((2, 2)), dma((2,)), dma((2,)), dma((2,)), dma((2,)),
        dma((2,)), dma((2,)), dma((2,)), dma((2, 2)), dma((2,)), dma((2, 4)),
    ]
    ig, wg = pl.pallas_call(
        body,
        out_shape=(
            pltpu.VMEM(field_shape, BF16),
            pltpu.VMEM(w_shape, F32),
        ),
        in_specs=[vmem, smem] + [vmem] * len(IN_VMEM) + [hbm] * (len(IN_HBM) + 3),
        out_specs=(vmem, vmem),
        scratch_shapes=scratch,
        compiler_params=pltpu.CompilerParams(
            collective_id=0, has_side_effects=True, vmem_limit_bytes=50 * 1024 * 1024
        ),
        cost_estimate=pl.CostEstimate(flops=10**10, bytes_accessed=2 * 10**7, transcendentals=0),
    )(
        point_weight, point_bias,
        *[tabs[name] for name in IN_VMEM],
        *[tabs[name] for name in IN_HBM],
        input_field.reshape(field_shape), cotangent.reshape(field_shape), spectral_weights,
    )
    return (ig.reshape(input_field.shape), wg)


def solution(mesh):
    return jax.shard_map(
        per_device,
        mesh=mesh,
        in_specs=(
            P(None, None, "gx", "gy", None),
            P(None, None, "gx", "gy", None),
            P(None, None, "gy", "gx", None),
            P(),
            P(),
        ),
        out_specs=(P(None, None, "gx", "gy", None), P(None, None, "gy", "gx", None)),
        check_vma=False,
    )
```

profile of v0, /device:TPU:1, one launch (start us, length us, event | category | flops | bytes accessed | tf_op | source)
XLA Modules:
  0.0 126.3 jit_solution(14364291886613457951)
XLA Ops:
  0.6 122.8 %shard_map.185 = (bf16[4,2,4,6,32,256]{5,4,3,2,1,0:T(8,128)(2,1)S(1)}, f32[2,17,6,2,1024]{4,3,2,1,0:T(2,128)S(1)}) custom-call(bf16[32,32]{1,0:T(8,128)(2,1)} %pw.1, f32[32]{0:T(128)} %bias.1, bf16[1024,256]{1,0:T(8,128)(2,1)} %constant.26.clone.wz, bf16[2,128,384]{2,1,0:T(8,128)(2,1)} %constant.28.clone.t1, bf16[512,32]{1,0:T(8,128)(2,1)} %constant.38.clone.a16, ...), custom_call_target="tpu_custom_call" | custom-call | flops 10000000000 | bytes 20000000 | tf_op jit(solution)/shard_map/pallas_call | solution.py:656
  123.4 1.7 %copy.22 = bf16[1,32,6,32,256]{4,3,2,1,0:T(8,128)(2,1)} copy(bf16[1,32,6,32,256]{4,3,2,1,0:T(8,128)(2,1)S(1)} %bitcast.3) | data formatting | bytes 6291456
  125.1 1.2 copy.23
where the time goes:
time: 126 us
  Pallas kernels  123 us (98%)
  local copies, waits for them, and re-layouts  2.84 us (2%)
    pallas_call x1, Pallas kernels, per_device(): pl.pallas_call(body, out_shape=(pltpu.VMEM(field_shape, BF16), pltpu.VMEM...  123 us
    unnamed x2, local copies, waits for them, and re-layouts  2.84 us

commit v1 on v0

--- a/solution.py
+++ b/solution.py
@@ -73,9 +73,9 @@
                 block = xt[:, :, :, :, :, :, i]
                 t2[:, :, zl_to, :, :, 2 * i + j, :, :, zl_to * 2 + j] = block.transpose(1, 4, 0, 5, 3, 2)
     fwd = t2.reshape(4, 8, 128, 384)
-    tabs["t2"] = np.concatenate(hi_lo(fwd), 3)
+    tabs["t2"] = hi_lo(fwd)[0]
     inv = t2.transpose(0, 6, 3, 7, 8, 1, 2, 4, 5).reshape(4, 6, 128, 512)
-    tabs["t2i"] = np.concatenate(hi_lo(inv), 2)
+    tabs["t2i"] = hi_lo(inv)[0]
     eye2, eye4 = np.eye(2), np.eye(4)
     ones16, ones32 = np.ones(16), np.ones(32)
     e1 = np.einsum("qr,cd,s,o->qcsrdo", eye2, eye4, ones16, ones32)
@@ -344,15 +344,14 @@
         mine = zh * 4 + zl
         for group in ((1, 2, 3, 4), (5, 6, 7, 8)):
             to = [lax.rem(mine + d, 8) for d in group]
-            values = xb[...]
-            out = mm(jnp.concatenate([t2[z] for z in to], 0), jnp.concatenate([values, values], 0))
+            out = mm(jnp.concatenate([t2[z] for z in to], 0), xb[...])
             for n, d in enumerate(group):
                 x_analysis_store(out[128 * n : 128 * n + 128], h, to[n])
                 for y in range(4 if d < 8 else 3):
                     c3(h, to[n], y if d < 8 else y_at(y + 1)).start()
         r3a[h, me] = rsb[h, me]
 
-    def analysis(first, second, received):
+    def analysis(first, middle, second, received):
         first()
         for h in range(2):
             for g in range(2):
@@ -361,6 +360,7 @@
                 for d in range(1, 8):
                     c2(h, s_at(d), g).start()
             r1[h, s] = vs[h, s]
+        middle()
         for h in range(2):
             all_of(r1, h, 7, s2r)
             x_analysis_load(h)
@@ -392,7 +392,7 @@
         for group in ((0, 1), (2, 3), (4, 5)):
             out = mm(jnp.concatenate([t2i[x] for x in group], 0), xb2[...])
             for n, x in enumerate(group):
-                part = out[256 * n : 256 * n + 128] + out[256 * n + 128 : 256 * n + 256]
+                part = out[128 * n : 128 * n + 128]
                 part = part[:64] + swap(part[64:], -1.0)
                 vs2[h, :, :, 128 * x : 128 * x + 128] = part[:, :128].reshape(8, 8, 128)
                 high, low = halves(part[:, 128:])
@@ -458,7 +458,7 @@
             all_of(vs2, h, 7, g2s)
             all_of(ys, h, 3, g1s)
 
-    def channel_map(wide, source):
+    def channel_matrix(wide):
         rows = row_of((512, 512))
         columns = slot_of((512, 512))
         full = lax.dot_general(
@@ -466,13 +466,14 @@
         )
         kron[...] = jnp.where(rows == columns, full, 0.0).astype(BF16)
 
+    def channel_map(source, low, high):
         def one(x):
             for at in (0, 16):
                 block = source[:, :, :, x, at : at + 16, :].reshape(512, 256)
                 out = mm(kron[...], block)
                 lin[:, :, :, x, at : at + 16, :] = out.reshape(4, 2, 4, 16, 256)
 
-        each(0, 6, one)
+        each(low, high, one)
 
     def lanes(b):
         return pl.ds(pl.multiple_of(b * 128, 128), 128)
@@ -578,30 +579,33 @@
             c1(h, to, g).start()
 
     def first_y_wait():
-        channel_map(mm(a16[...], pw[...]), f)
-        loads[1].wait()
-
-    def first_z_wait():
         weights_in()
         acc[...] = jnp.zeros_like(acc)
+        loads[1].wait()
+
+    def second_x_wait():
+        wide = lax.dot_general(a16[...], pw[...], (((1,), (1,)), ((), ())), preferred_element_type=F32)
+        channel_matrix(wide)
+        channel_map(pg, 0, 3)
 
     def second_z_wait():
-        wide = lax.dot_general(a16[...], pw[...], (((1,), (1,)), ((), ())), preferred_element_type=F32)
-        channel_map(wide, pg)
+        channel_map(pg, 3, 6)
         gexp[...] = jnp.zeros_like(gexp)
 
-    def wait_loads():
+    def first_gather_wait():
+        channel_matrix(mm(a16[...], pw[...]))
+        channel_map(f, 0, 6)
         for load in loads[3:]:
             load.wait()
 
     for h in range(2):
         analysis_start(f, h, h == 1)
-    analysis(first_y_wait, first_z_wait, mix_one)
+    analysis(first_y_wait, lambda: None, lambda: None, mix_one)
     loads[2].wait()
     mix_two()
     analysis_end()
-    synthesis(wait_loads, finish_pre, second_own, second_start)
-    analysis(lambda: None, second_z_wait, back_one)
+    synthesis(first_gather_wait, finish_pre, second_own, second_start)
+    analysis(lambda: None, second_x_wait, second_z_wait, back_one)
     back_two()
     synthesis(weight_grad, finish_grad, lambda h: None, lambda h, fr: None)
     analysis_end()
@@ -616,8 +620,8 @@
     hbm = pl.BlockSpec(memory_space=pl.ANY)
     dma = pltpu.SemaphoreType.DMA
     scratch = [
-        pltpu.VMEM((8, 128, 768), BF16),
-        pltpu.VMEM((6, 256, 512), BF16),
+        pltpu.VMEM((8, 128, 384), BF16),
+        pltpu.VMEM((6, 128, 512), BF16),
         pltpu.VMEM((4, 256, 256), BF16),
         pltpu.VMEM((8, 128, 256), BF16),
         pltpu.VMEM((2, 2, 256, 256), BF16),

time: 126 us -> 127 us (level)
  no operation moved by 1% of the time
where the time goes in v1:
time: 127 us
  Pallas kernels  123 us (97%)
  local copies, waits for them, and re-layouts  2.84 us (2%)
    pallas_call x1, Pallas kernels, per_device(): pl.pallas_call(body, out_shape=(pltpu.VMEM(field_shape, BF16), pltpu.VMEM...  123 us
    unnamed x2, local copies, waits for them, and re-layouts  2.84 us

profile of v1, /device:TPU:1, one launch (start us, length us, event | category | flops | bytes accessed | tf_op | source)
XLA Modules:
  0.0 126.9 jit_solution(1718512000780120138)
XLA Ops:
  0.6 123.5 %shard_map.185 = (bf16[4,2,4,6,32,256]{5,4,3,2,1,0:T(8,128)(2,1)S(1)}, f32[2,17,6,2,1024]{4,3,2,1,0:T(2,128)S(1)}) custom-call(bf16[32,32]{1,0:T(8,128)(2,1)} %pw.1, f32[32]{0:T(128)} %bias.1, bf16[1024,256]{1,0:T(8,128)(2,1)} %constant.26.clone.wz, bf16[2,128,384]{2,1,0:T(8,128)(2,1)} %constant.28.clone.t1, bf16[512,32]{1,0:T(8,128)(2,1)} %constant.38.clone.a16, ...), custom_call_target="tpu_custom_call" | custom-call | flops 10000000000 | bytes 20000000 | tf_op jit(solution)/shard_map/pallas_call | solution.py:660
  124.1 1.7 %copy.22 = bf16[1,32,6,32,256]{4,3,2,1,0:T(8,128)(2,1)} copy(bf16[1,32,6,32,256]{4,3,2,1,0:T(8,128)(2,1)S(1)} %bitcast.3) | data formatting | bytes 6291456
  125.8 1.2 copy.23

commit v2 on v1

--- a/solution.py
+++ b/solution.py
@@ -351,7 +351,7 @@
                     c3(h, to[n], y if d < 8 else y_at(y + 1)).start()
         r3a[h, me] = rsb[h, me]
 
-    def analysis(first, middle, second, received):
+    def analysis(first, second, received):
         first()
         for h in range(2):
             for g in range(2):
@@ -360,7 +360,6 @@
                 for d in range(1, 8):
                     c2(h, s_at(d), g).start()
             r1[h, s] = vs[h, s]
-        middle()
         for h in range(2):
             all_of(r1, h, 7, s2r)
             x_analysis_load(h)
@@ -579,33 +578,32 @@
             c1(h, to, g).start()
 
     def first_y_wait():
+        channel_matrix(mm(a16[...], pw[...]))
+        channel_map(f, 0, 6)
+        loads[1].wait()
+
+    def first_z_wait():
         weights_in()
         acc[...] = jnp.zeros_like(acc)
-        loads[1].wait()
-
-    def second_x_wait():
+
+    def second_z_wait():
         wide = lax.dot_general(a16[...], pw[...], (((1,), (1,)), ((), ())), preferred_element_type=F32)
         channel_matrix(wide)
-        channel_map(pg, 0, 3)
-
-    def second_z_wait():
-        channel_map(pg, 3, 6)
+        channel_map(pg, 0, 6)
         gexp[...] = jnp.zeros_like(gexp)
 
-    def first_gather_wait():
-        channel_matrix(mm(a16[...], pw[...]))
-        channel_map(f, 0, 6)
+    def wait_loads():
         for load in loads[3:]:
             load.wait()
 
     for h in range(2):
         analysis_start(f, h, h == 1)
-    analysis(first_y_wait, lambda: None, lambda: None, mix_one)
+    analysis(first_y_wait, first_z_wait, mix_one)
     loads[2].wait()
     mix_two()
     analysis_end()
-    synthesis(first_gather_wait, finish_pre, second_own, second_start)
-    analysis(lambda: None, second_x_wait, second_z_wait, back_one)
+    synthesis(wait_loads, finish_pre, second_own, second_start)
+    analysis(lambda: None, second_z_wait, back_one)
     back_two()
     synthesis(weight_grad, finish_grad, lambda h: None, lambda h, fr: None)
     analysis_end()

time: 127 us -> 125 us (0.984)
    pallas_call x1, Pallas kernels: 123 us -> 122 us  [per_device(): pl.pallas_call(body, out_shape=(pltpu.VMEM(field_shape, BF16), pltpu.VMEM...]
where the time goes in v2:
time: 125 us
  Pallas kernels  122 us (98%)
  local copies, waits for them, and re-layouts  2.84 us (2%)
    pallas_call x1, Pallas kernels, per_device(): pl.pallas_call(body, out_shape=(pltpu.VMEM(field_shape, BF16), pltpu.VMEM...  122 us
    unnamed x2, local copies, waits for them, and re-layouts  2.84 us

profile of v2, /device:TPU:1, one launch (start us, length us, event | category | flops | bytes accessed | tf_op | source)
XLA Modules:
  0.0 125.2 jit_solution(16634064152116742788)
XLA Ops:
  0.6 121.7 %shard_map.185 = (bf16[4,2,4,6,32,256]{5,4,3,2,1,0:T(8,128)(2,1)S(1)}, f32[2,17,6,2,1024]{4,3,2,1,0:T(2,128)S(1)}) custom-call(bf16[32,32]{1,0:T(8,128)(2,1)} %pw.1, f32[32]{0:T(128)} %bias.1, bf16[1024,256]{1,0:T(8,128)(2,1)} %constant.26.clone.wz, bf16[2,128,384]{2,1,0:T(8,128)(2,1)} %constant.28.clone.t1, bf16[512,32]{1,0:T(8,128)(2,1)} %constant.38.clone.a16, ...), custom_call_target="tpu_custom_call" | custom-call | flops 10000000000 | bytes 20000000 | tf_op jit(solution)/shard_map/pallas_call | solution.py:658
  122.4 1.7 %copy.22 = bf16[1,32,6,32,256]{4,3,2,1,0:T(8,128)(2,1)} copy(bf16[1,32,6,32,256]{4,3,2,1,0:T(8,128)(2,1)S(1)} %bitcast.3) | data formatting | bytes 6291456
  124.1 1.2 copy.23

commit v3 on v2

--- a/solution.py
+++ b/solution.py
@@ -475,7 +475,11 @@
         each(low, high, one)
 
     def lanes(b):
-        return pl.ds(pl.multiple_of(b * 128, 128), 128)
+        return pl.ds(b * 128, 128) if isinstance(b, int) else pl.ds(pl.multiple_of(b * 128, 128), 128)
+
+    def unrolled(count, fn):
+        for y in range(count):
+            fn(y)
 
     def weights_in():
         loads[0].wait()
@@ -509,7 +513,7 @@
             acc[:, :128] += w_real * real - w_imag * imag
             acc[:, 128:] += w_real * imag + w_imag * real
 
-        each(0, 4, one)
+        unrolled(4, one)
 
     def spread_out(h, y):
         def one(z):
@@ -535,7 +539,7 @@
         def one(y):
             gexp[...] += split_left(spread_rows(md[h, y]), e2[2 * y + h])
 
-        each(0, 4, one)
+        unrolled(4, one)
 
     def back_two():
         for h in range(2):
@@ -549,7 +553,7 @@
                 mq[h, y] = gather_rows(split_left(jnp.concatenate([real, imag], 1), r2[...]))
                 spread_out(h, y)
 
-            each(0, 4, two)
+            unrolled(4, two)
             keep_own(h)
 
     def weight_grad():

time: 125 us -> 125 us (level)
  no operation moved by 1% of the time
where the time goes in v3:
time: 125 us; the launch traced here: 124 us
  Pallas kernels  121 us (97%)
  local copies, waits for them, and re-layouts  2.84 us (2%)
    pallas_call x1, Pallas kernels, per_device(): pl.pallas_call(body, out_shape=(pltpu.VMEM(field_shape, BF16), pltpu.VMEM...  121 us
    unnamed x2, local copies, waits for them, and re-layouts  2.84 us

profile of v3, /device:TPU:1, one launch (start us, length us, event | category | flops | bytes accessed | tf_op | source)
XLA Modules:
  0.0 124.4 jit_solution(7502108788786920771)
XLA Ops:
  0.6 120.9 %shard_map.185 = (bf16[4,2,4,6,32,256]{5,4,3,2,1,0:T(8,128)(2,1)S(1)}, f32[2,17,6,2,1024]{4,3,2,1,0:T(2,128)S(1)}) custom-call(bf16[32,32]{1,0:T(8,128)(2,1)} %pw.1, f32[32]{0:T(128)} %bias.1, bf16[1024,256]{1,0:T(8,128)(2,1)} %constant.26.clone.wz, bf16[2,128,384]{2,1,0:T(8,128)(2,1)} %constant.28.clone.t1, bf16[512,32]{1,0:T(8,128)(2,1)} %constant.38.clone.a16, ...), custom_call_target="tpu_custom_call" | custom-call | flops 10000000000 | bytes 20000000 | tf_op jit(solution)/shard_map/pallas_call | solution.py:662
  121.6 1.7 %copy.22 = bf16[1,32,6,32,256]{4,3,2,1,0:T(8,128)(2,1)} copy(bf16[1,32,6,32,256]{4,3,2,1,0:T(8,128)(2,1)S(1)} %bitcast.3) | data formatting | bytes 6291456
  123.3 1.2 copy.23
